TPU v7x, 512 devices: a whole 4x8x8 slice. The times are simulated.
512 devices in a mesh: language: 8 (over y_hi, core), fsdp: 64 (over y_lo, x, z).
Axes of the slice: x: 4, y: 8 (y_hi: 4, y_lo: 2; y = y_hi * 2 + y_lo), z: 8, core: 2. Of those that a mesh axis runs over, the one named last changes fastest.
Arguments:
- hidden: bfloat16 [16, 8192, 5120], P('language', 'fsdp'), may hold values from -60 to 60
- latent_grad: bfloat16 [16, 8192, 64], P('language', 'fsdp'), may hold values from -0.15625 to 0.15625
- lang_ids: int32 [16], P('language'), may hold values from 0 to 15, each once
- old_weights: float32 [16], replicated, may hold values from 0.02 to 0.2
- param: float32 [5120, 64], P('fsdp'), may hold values from -6 to 6
- first_moment: float32 [5120, 64], P('fsdp'), may hold values from -6 to 6
- second_moment: float32 [5120, 64], P('fsdp'), may hold values from 0.25 to 4
Outputs:
- new_param: float32 [5120, 64], P('fsdp')
- new_first: float32 [5120, 64], P('fsdp')
- new_second: float32 [5120, 64], P('fsdp')
- new_logweights: float32 [16], replicated
Inputs may be any that keep to these rules, and one draw needn't show every extreme that they name: `lang_ids`: each id appears in exactly one slot.
All inputs are finite; a program needn't handle non-finite values.
Results may differ from a plain program's by a relative error of at most 0.0003.
Values may be sent and summed in bfloat16 or wider, within the bound.
A program may use at most 64 MiB of HBM per device.

v0:
```python
import jax
import jax.numpy as jnp
from jax import lax
from jax.sharding import PartitionSpec as P

STEP = 100


def log_weights(by_lang, square, old_weights):
    logits = jnp.log(old_weights) + old_weights.shape[0] * (by_lang / (square + 1e-06))
    return logits - jnp.log(jnp.sum(jnp.exp(logits)))


def local(hidden, latent_grad, lang_ids, old_weights, param, first_moment, second_moment):
    langs = old_weights.shape[0]
    slot_grad = lax.psum_scatter(
        jnp.einsum("ltd,ltr->dlr", hidden, latent_grad, preferred_element_type=jnp.float32),
        "fsdp",
        scatter_dimension=0,
        tiled=True,
    )
    onehot = (lang_ids[:, None] == jnp.arange(langs, dtype=jnp.int32)[None, :]).astype(jnp.float32)
    total = lax.psum(jnp.sum(slot_grad, axis=1), "language")
    dots = jnp.einsum("dlr,dr->l", slot_grad, total, precision=lax.Precision.HIGHEST)
    leader = (lax.axis_index("language") == 0).astype(jnp.float32)
    square_part = jnp.sum(total * total) * leader
    by_lang_part = jnp.dot(dots, onehot, precision=lax.Precision.HIGHEST)
    by_lang, square = lax.psum((by_lang_part, square_part), ("language", "fsdp"))
    new_logweights = log_weights(by_lang, square, old_weights)
    weights = jnp.exp(new_logweights)
    slot_weight = jnp.dot(onehot, weights, precision=lax.Precision.HIGHEST)
    local_update = jnp.einsum("l,dlr->dr", slot_weight, slot_grad, precision=lax.Precision.HIGHEST)
    update = lax.psum(local_update, "language")
    new_first = 0.9 * first_moment + 0.1 * update
    new_second = 0.95 * second_moment + 0.05 * update * update
    first_hat = new_first / (1.0 - 0.9**STEP)
    second_hat = new_second / (1.0 - 0.95**STEP)
    new_param = param - 0.02 * (first_hat / (jnp.sqrt(second_hat) + 1e-08) + 0.1 * param)
    return (new_param, new_first, new_second, new_logweights)


def solution(mesh):
    placed = (
        P("language", "fsdp", None),
        P("language", "fsdp", None),
        P("language"),
        P(),
        P("fsdp", None),
        P("fsdp", None),
        P("fsdp", None),
    )
    return jax.shard_map(
        local,
        mesh=mesh,
        in_specs=placed,
        out_specs=(P("fsdp", None), P("fsdp", None), P("fsdp", None), P()),
        check_vma=False,
    )
```

profile of v0, /device:TPU:2, one launch (start us, length us, event | category | flops | bytes accessed | tf_op | source)
XLA Modules:
  0.0 505.8 jit_solution(7632736756905314304)
XLA Ops:
  7.2 0.0 copy-start
  7.2 0.0 reduce-scatter.4.cloned.1.call-start
  7.2 1.7 copy-done
  8.9 2.8 fusion.7
  11.7 3.2 copy.16
  14.9 0.0 copy-start.5
  14.9 0.0 copy-start.4
  14.9 0.0 copy-start.1
  14.9 0.0 copy-start.2
  14.9 0.0 copy-start.3
  14.9 0.0 reduce-scatter.4.cloned.1.call-update
  15.0 310.9 %reduce-scatter.4.cloned.1.call-done = f32[80,128]{1,0:T(8,128)} async-done(((f32[5120,128]{1,0:T(8,128)}), f32[80,128]{1,0:T(8,128)}) %reduce-scatter.4.cloned.1.call-update) | async-done | bytes 40976
  325.9 0.9 copy.17
  326.8 27.2 %psum.28 = f32[80,64]{0,1:T(8,128)S(1)} all-reduce(f32[80,64]{0,1:T(8,128)S(1)} %reduce_sum.27), channel_id=1, replica_groups=mesh['language'=8,'fsdp'=64] {'language'}, use_global_device_ids=true, to_apply=%region_2.0 | all-reduce | flops 5120 | bytes 40960 | tf_op jit(solution)/shard_map/psum | solution.py:23
  354.0 0.6 multiply_reduce_fusion
  354.6 0.7 convolution_bitcast_fusion.2
  355.3 0.0 copy-done.5
  355.3 0.2 convolution_bitcast_fusion.1
  356.1 111.2 %all-reduce = (f32[16]{0:T(128)S(1)}, f32[]{:T(128)}) all-reduce(f32[16]{0:T(128)S(1)} %convolution_bitcast_fusion.1, f32[]{:T(128)S(6)} %mul.45), channel_id=1, replica_groups=mesh['language'=8,'fsdp'=64] {'language','fsdp'}, use_global_device_ids=true, to_apply=%region_3.0 | all-reduce | flops 17 | bytes 136 | tf_op jit(solution)/shard_map/psum | solution.py:28
  468.0 0.0 copy-done.4
  468.0 0.6 exponential_reduce_fusion
  469.3 0.0 copy-start.6
  469.3 0.2 convolution_bitcast_fusion
  469.5 0.4 fusion
  469.9 28.4 %psum.31 = f32[80,64]{0,1:T(8,128)S(1)} all-reduce(f32[80,64]{0,1:T(8,128)S(1)} %bitcast.34), channel_id=1, replica_groups=mesh['language'=8,'fsdp'=64] {'language'}, use_global_device_ids=true, to_apply=%region_7.0 | all-reduce | flops 5120 | bytes 40960 | tf_op jit(solution)/shard_map/psum | solution.py:33
  498.3 0.0 copy-done.1
  498.3 0.0 copy-done.2
  498.3 0.0 copy-done.3
  498.3 0.7 multiply_subtract_fusion
  499.0 0.0 copy-done.6
  (2 shorter events, 0.0 us)
Async XLA Ops:
  7.2 1.7 copy-start
  7.2 318.7 %reduce-scatter.4.cloned.1.call-start = ((), (), s32[]{:S(2)}) async-start(), calls=%async_computation.1 | async-start | bytes 2662400
  14.9 340.3 %copy-start.5 = (s32[2]{0:T(128)S(1)}, s32[2]{0:T(128)}, u32[]{:S(2)}) copy-start(s32[2]{0:T(128)} %param.9) | copy-start | bytes 28
  14.9 453.1 %copy-start.4 = (f32[16]{0:T(128)S(1)}, f32[16]{0:T(128)}, u32[]{:S(2)}) copy-start(f32[16]{0:T(128)} %param.10) | copy-start | bytes 196
  14.9 483.4 %copy-start.1 = (f32[80,64]{0,1:T(8,128)S(1)}, f32[80,64]{0,1:T(8,128)}, u32[]{:S(2)}) copy-start(f32[80,64]{0,1:T(8,128)} %param.11) | copy-start | bytes 61444
  14.9 483.4 %copy-start.2 = (f32[80,64]{0,1:T(8,128)S(1)}, f32[80,64]{0,1:T(8,128)}, u32[]{:S(2)}) copy-start(f32[80,64]{0,1:T(8,128)} %param.12) | copy-start | bytes 61444
  14.9 483.4 %copy-start.3 = (f32[80,64]{0,1:T(8,128)S(1)}, f32[80,64]{0,1:T(8,128)}, u32[]{:S(2)}) copy-start(f32[80,64]{0,1:T(8,128)} %param.13) | copy-start | bytes 61444
  469.3 29.7 %copy-start.6 = (f32[16]{0:T(128)}, f32[16]{0:T(128)S(1)}, u32[]{:S(2)}) copy-start(f32[16]{0:T(128)S(1)} %broadcast_subtract_fusion) | copy-start | bytes 196
Sparse Core Ops, SparseCore 0:
  15.1 310.7 reduce-scatter.3
where the time goes:
time: 506 us
  waiting for transfers between devices  311 us (61%)
  blocking collectives  167 us (33%)
  between operations  16.1 us (3%)
  local copies, waits for them, and re-layouts  5.81 us (1%)
    unnamed x2, waiting for transfers between devices  311 us
    psum x1, blocking collectives, local(): lax.psum((by_lang_part, square_part), ('language', 'fsdp'))  111 us
    psum x1, blocking collectives, local(): update = lax.psum(local_update, 'language')  28.4 us
    psum x1, blocking collectives, local(): total = lax.psum(jnp.sum(slot_grad, axis=1), 'language')  27.2 us
  transfers between devices with their start and end apart: 1, of which 1 were waited for; matrix products, arithmetic and copies ran while one was open for 0% of the time, Pallas kernels for 0%

commit v1 on v0

--- a/solution.py
+++ b/solution.py
@@ -2,6 +2,7 @@
 import jax.numpy as jnp
 from jax import lax
 from jax.sharding import PartitionSpec as P
+from jax.lax import psum
 
 STEP = 100
 
@@ -12,6 +13,10 @@
 
 
 def local(hidden, latent_grad, lang_ids, old_weights, param, first_moment, second_moment):
+
+    def hold_scales_up(inp):
+        return psum(psum(inp, axis_name="language"), axis_name="fsdp")
+
     langs = old_weights.shape[0]
     slot_grad = lax.psum_scatter(
         jnp.einsum("ltd,ltr->dlr", hidden, latent_grad, preferred_element_type=jnp.float32),
@@ -25,7 +30,7 @@
     leader = (lax.axis_index("language") == 0).astype(jnp.float32)
     square_part = jnp.sum(total * total) * leader
     by_lang_part = jnp.dot(dots, onehot, precision=lax.Precision.HIGHEST)
-    by_lang, square = lax.psum((by_lang_part, square_part), ("language", "fsdp"))
+    by_lang, square = hold_scales_up((by_lang_part, square_part))
     new_logweights = log_weights(by_lang, square, old_weights)
     weights = jnp.exp(new_logweights)
     slot_weight = jnp.dot(onehot, weights, precision=lax.Precision.HIGHEST)

time: 506 us -> 578 us (1.14)
  the two profiles are of different devices: /device:TPU:2 before, /device:TPU:40 now
where the time goes in v1:
time: 578 us
  waiting for transfers between devices  327 us (57%)
  blocking collectives  223 us (39%)
  between operations  16.1 us (3%)
  local copies, waits for them, and re-layouts  5.81 us (1%)
    unnamed x2, waiting for transfers between devices  327 us
    psum x2, blocking collectives, hold_scales_up(): return psum(psum(inp, axis_name='language'), axis_name='fsdp')  169 us
    psum x1, blocking collectives, local(): update = lax.psum(local_update, 'language')  27.2 us
    psum x1, blocking collectives, local(): total = lax.psum(jnp.sum(slot_grad, axis=1), 'language')  27.2 us
  transfers between devices with their start and end apart: 1, of which 1 were waited for; matrix products, arithmetic and copies ran while one was open for 0% of the time, Pallas kernels for 0%

profile of v1, /device:TPU:40, one launch (start us, length us, event | category | flops | bytes accessed | tf_op | source)
XLA Modules:
  0.0 577.8 jit_solution(12708192756847903330)
XLA Ops:
  7.2 0.0 copy-start
  7.2 0.0 reduce-scatter.4.cloned.1.call-start
  7.2 1.7 copy-done
  8.9 2.8 fusion.7
  11.7 3.2 copy.16
  14.9 0.0 copy-start.5
  14.9 0.0 copy-start.4
  14.9 0.0 copy-start.1
  14.9 0.0 copy-start.2
  14.9 0.0 copy-start.3
  14.9 0.0 reduce-scatter.4.cloned.1.call-update
  15.0 326.5 %reduce-scatter.4.cloned.1.call-done = f32[80,128]{1,0:T(8,128)} async-done(((f32[5120,128]{1,0:T(8,128)}), f32[80,128]{1,0:T(8,128)}) %reduce-scatter.4.cloned.1.call-update) | async-done | bytes 40976
  341.5 0.9 copy.17
  342.4 27.2 %psum.42 = f32[80,64]{0,1:T(8,128)S(1)} all-reduce(f32[80,64]{0,1:T(8,128)S(1)} %reduce_sum.27), channel_id=1, replica_groups=mesh['language'=8,'fsdp'=64] {'language'}, use_global_device_ids=true, to_apply=%region_2.0 | all-reduce | flops 5120 | bytes 40960 | tf_op jit(solution)/shard_map/psum | solution.py:28
  369.6 0.6 multiply_reduce_fusion
  370.2 0.7 convolution_bitcast_fusion.2
  370.9 0.0 copy-done.5
  370.9 0.2 convolution_bitcast_fusion.1
  371.7 14.7 %all-reduce.1 = (f32[16]{0:T(128)S(1)}, f32[]{:T(128)}) all-reduce(f32[16]{0:T(128)S(1)} %convolution_bitcast_fusion.1, f32[]{:T(128)S(6)} %mul.45), channel_id=1, replica_groups=mesh['language'=8,'fsdp'=64] {'language'}, use_global_device_ids=true, to_apply=%region_3.0 | all-reduce | flops 17 | bytes 136 | tf_op jit(solution)/shard_map/psum | solution.py:18
  386.5 154.1 %all-reduce = (f32[16]{0:T(128)S(1)}, f32[]{:T(128)}) all-reduce(f32[16]{0:T(128)S(1)} %get-tuple-element.6, f32[]{:T(128)} %get-tuple-element.7), channel_id=1, replica_groups=mesh['language'=8,'fsdp'=64] {'fsdp'}, use_global_device_ids=true, to_apply=%region_4.0 | all-reduce | flops 17 | bytes 136 | tf_op jit(solution)/shard_map/psum | solution.py:18
  541.2 0.0 copy-done.4
  541.2 0.6 exponential_reduce_fusion
  542.5 0.0 copy-start.6
  542.5 0.2 convolution_bitcast_fusion
  542.7 0.4 fusion
  543.1 27.2 %psum.47 = f32[80,64]{0,1:T(8,128)S(1)} all-reduce(f32[80,64]{0,1:T(8,128)S(1)} %bitcast.34), channel_id=1, replica_groups=mesh['language'=8,'fsdp'=64] {'language'}, use_global_device_ids=true, to_apply=%region_9.0 | all-reduce | flops 5120 | bytes 40960 | tf_op jit(solution)/shard_map/psum | solution.py:38
  570.3 0.0 copy-done.1
  570.3 0.0 copy-done.2
  570.3 0.0 copy-done.3
  570.3 0.7 multiply_subtract_fusion
  571.0 0.0 copy-done.6
  (2 shorter events, 0.0 us)
Async XLA Ops:
  7.2 1.7 copy-start
  7.2 334.3 %reduce-scatter.4.cloned.1.call-start = ((), (), s32[]{:S(2)}) async-start(), calls=%async_computation.1 | async-start | bytes 2662400
  14.9 356.0 %copy-start.5 = (s32[2]{0:T(128)S(1)}, s32[2]{0:T(128)}, u32[]{:S(2)}) copy-start(s32[2]{0:T(128)} %param.9) | copy-start | bytes 28
  14.9 526.3 %copy-start.4 = (f32[16]{0:T(128)S(1)}, f32[16]{0:T(128)}, u32[]{:S(2)}) copy-start(f32[16]{0:T(128)} %param.10) | copy-start | bytes 196
  14.9 555.4 %copy-start.1 = (f32[80,64]{0,1:T(8,128)S(1)}, f32[80,64]{0,1:T(8,128)}, u32[]{:S(2)}) copy-start(f32[80,64]{0,1:T(8,128)} %param.11) | copy-start | bytes 61444
  14.9 555.4 %copy-start.2 = (f32[80,64]{0,1:T(8,128)S(1)}, f32[80,64]{0,1:T(8,128)}, u32[]{:S(2)}) copy-start(f32[80,64]{0,1:T(8,128)} %param.12) | copy-start | bytes 61444
  14.9 555.3 %copy-start.3 = (f32[80,64]{0,1:T(8,128)S(1)}, f32[80,64]{0,1:T(8,128)}, u32[]{:S(2)}) copy-start(f32[80,64]{0,1:T(8,128)} %param.13) | copy-start | bytes 61444
  542.5 28.4 %copy-start.6 = (f32[16]{0:T(128)}, f32[16]{0:T(128)S(1)}, u32[]{:S(2)}) copy-start(f32[16]{0:T(128)S(1)} %broadcast_subtract_fusion) | copy-start | bytes 196
Sparse Core Ops, SparseCore 0:
  15.1 326.3 reduce-scatter.3
